TPU v7x, 256 devices: a whole 4x4x8 slice. The times are simulated.
256 devices in a mesh: wide: 32 (over z, y_lo, core), narrow: 8 (over y_hi, x).
Axes of the slice: x: 4, y: 4 (y_hi: 2, y_lo: 2; y = y_hi * 2 + y_lo), z: 8, core: 2. Of those that a mesh axis runs over, the one named last changes fastest.
Arguments:
- tokens: bfloat16 [64, 2048, 3072], P('wide', 'narrow'), may hold values from -6 to 6
- gain: float32 [3072], replicated, may hold values from 0.25 to 1.75
- w_qkv: bfloat16 [3072, 4608], P(None, 'narrow'), may hold values from -2 to 2
- band: int32 [12], replicated, may hold values from 8 to 63
Outputs:
- attended: bfloat16 [64, 2048, 1536], P('wide', 'narrow')
Inputs may be any that keep to these rules, and one draw needn't show every extreme that they name: A key frame u is used for query frame t in head h when |t - u| <= band[h].
All inputs are finite; a program needn't handle non-finite values.
Results may differ from a plain program's by a relative error of at most 0.0082.
Values may be sent and summed in bfloat16 or wider, within the bound.
No kernel may reach another device: no remote copies, remote signals or barrier semaphores. Data moves between devices by JAX's collectives and lax.ppermute only.
A program may use at most 128 MiB of HBM per device.

v0:
```python
import math

import jax
import jax.numpy as jnp
from jax import lax
from jax.sharding import PartitionSpec as P

HEADS = 12
HD = 128
INNER = 1536


EPS = 1e-06


def normalize(tokens, gain):
    values = tokens.astype(jnp.float32)
    centered = values - jnp.mean(values, axis=-1, keepdims=True)
    spread = jnp.mean(centered * centered, axis=-1, keepdims=True)
    return (centered * lax.rsqrt(spread + EPS) * gain).astype(jnp.bfloat16)


def temporal(qkv, band):
    frames, count = (qkv.shape[0], qkv.shape[1])
    query = qkv[..., :INNER].reshape(frames, count, HEADS, HD)
    keys = qkv[..., INNER : 2 * INNER].reshape(frames, count, HEADS, HD)
    values = qkv[..., 2 * INNER :].reshape(frames, count, HEADS, HD)
    scores = jnp.einsum("tbhe,ubhe->bhtu", query, keys, preferred_element_type=jnp.float32) * (
        1.0 / math.sqrt(HD)
    )
    steps_t = jnp.arange(frames, dtype=jnp.int32)
    distance = jnp.abs(steps_t[:, None] - steps_t[None, :])
    allowed = distance[None, None, :, :] <= band[None, :, None, None]
    scores = jnp.where(allowed, scores, -jnp.inf)
    highest = jnp.max(scores, axis=-1, keepdims=True)
    weights = jnp.exp(scores - highest)
    total = jnp.sum(weights, axis=-1, keepdims=True)
    probs = (weights / total).astype(jnp.bfloat16)
    result = jnp.einsum("bhtu,ubhe->tbhe", probs, values, preferred_element_type=jnp.float32)
    return result.astype(jnp.bfloat16).reshape(frames, count, INNER)


def per_device(tokens, gain, w_qkv, band):
    normed = normalize(tokens, gain)
    moved = lax.all_to_all(normed, "wide", split_axis=1, concat_axis=0, tiled=True)
    frames, positions, width = moved.shape
    piece = lax.all_gather(w_qkv, "narrow", axis=1, tiled=True)
    product = jnp.dot(moved.reshape(-1, width), piece, preferred_element_type=jnp.float32)
    qkv = product.astype(jnp.bfloat16).reshape(frames, positions, piece.shape[1])
    result = temporal(qkv, band)
    return lax.all_to_all(result, "wide", split_axis=0, concat_axis=1, tiled=True)


def solution(mesh):
    placed = (P("wide", "narrow", None), P(), P(None, "narrow"), P())
    return jax.shard_map(
        per_device, mesh=mesh, in_specs=placed, out_specs=P("wide", "narrow", None), check_vma=False
    )
```

profile of v0, /device:TPU:1, one launch (start us, length us, event | category | flops | bytes accessed | tf_op | source)
XLA Modules:
  0.0 424.7 jit_solution(6936479745839639179)
XLA Ops:
  6.5 0.0 copy-start
  6.5 0.0 all-gather.2.cloned.1.call-start
  6.5 0.7 all-gather.2.cloned.1.call-update
  7.3 1.2 copy-done
  8.4 0.0 copy-start.1
  8.4 2.9 convert_reduce_fusion
  11.3 4.6 %fusion.4 = f32[2,256]{0,1:T(8,128)S(1)} fusion(f32[2,256]{0,1:T(8,128)S(1)} %broadcast_multiply_fusion, bf16[2,256,3072]{2,1,0:T(8,128)(2,1)S(1)} %copy-done), kind=kLoop, calls=%fused_computation.7 | loop fusion | flops 6290944 | bytes 3149824 | tf_op jit(solution)/shard_map/reduce_sum | solution.py:19
  16.0 0.0 copy-done.1
  16.0 12.4 %fusion.6 = bf16[2,256,3072]{2,0,1:T(2,128)(2,1)} fusion(f32[3072]{0:T(1024)S(1)} %copy-done.1, f32[2,256]{0,1:T(8,128)S(1)} %add_rsqrt_fusion, f32[2,256]{0,1:T(8,128)S(1)} %broadcast_multiply_fusion, bf16[2,256,3072]{2,1,0:T(8,128)(2,1)S(1)} %copy-done), kind=kLoop, calls=%fused_computation.9 | loop fusion | flops 7864320 | bytes 6307840 | tf_op jit(solution)/shard_map/convert_element_type | solution.py:20
  28.4 11.3 %all-to-all-start = ((bf16[2,256,3072]{2,0,1:T(2,128)(2,1)}), bf16[2,256,3072]{2,0,1:T(2,128)(2,1)S(1)}, u32[]{:S(2)}, u32[]{:S(2)}) async-start(bf16[2,256,3072]{2,0,1:T(2,128)(2,1)} %fusion.6), calls=%async_computation | async-start | bytes 6291456 | tf_op jit(solution)/shard_map/all_to_all | solution.py:45
  39.7 0.0 copy-done.2
  39.7 0.1 broadcast_compare_fusion
  39.8 71.7 %all-to-all-done = bf16[2,256,3072]{2,0,1:T(2,128)(2,1)S(1)} async-done(((bf16[2,256,3072]{2,0,1:T(2,128)(2,1)}), bf16[2,256,3072]{2,0,1:T(2,128)(2,1)S(1)}, u32[]{:S(2)}, u32[]{:S(2)}) %all-to-all-start) | async-done | bytes 3145760 | tf_op jit(solution)/shard_map/all_to_all | solution.py:45
  111.5 0.8 copy.42
  112.3 0.3 copy.20
  112.6 231.0 %all-gather.2.cloned.1.call-done = bf16[3072,4608]{0,1:T(8,128)(2,1)} async-done(((bf16[3072,576]{0,1:T(8,128)(2,1)}), bf16[3072,4608]{0,1:T(8,128)(2,1)}) %all-gather.2.cloned.1.call-update) | async-done | bytes 28311568 | tf_op jit(solution)/shard_map/all_gather | solution.py:47
  343.6 18.9 %fusion.1 = bf16[64,8,4608]{2,1,0:T(8,128)(2,1)S(1)} fusion(bf16[512,3072]{1,0:T(8,128)(2,1)S(1)} %bitcast.30, bf16[3072,4608]{0,1:T(8,128)(2,1)} %all-gather.2.cloned.1.call-done), kind=kOutput, calls=%fused_computation.4 | convolution fusion | flops 14497873920 | bytes 36175872 | tf_op jit(solution)/shard_map/dot_general | solution.py:48
  362.5 0.8 slice_bitcast_fusion.2
  363.3 2.0 fusion.9
  365.3 1.3 fusion.21
  366.6 1.3 fusion.16
  367.9 1.0 copy.44
  368.9 47.8 %all_to_all.33 = bf16[64,8,1536]{2,1,0:T(8,128)(2,1)S(1)} all-to-all(bf16[64,8,1536]{2,1,0:T(8,128)(2,1)S(1)} %bitcast.28), channel_id=1, replica_groups=mesh['wide'=32,'narrow'=8] {'wide'}, dimensions={0} | all-to-all | bytes 3145728 | tf_op jit(solution)/shard_map/all_to_all | solution.py:51
  416.6 1.2 copy.43
  (4 shorter events, 0.1 us)
Async XLA Ops:
  6.5 1.9 copy-start
  6.5 337.0 %all-gather.2.cloned.1.call-start = ((), (), s32[]{:S(2)}) async-start(), calls=%async_computation.2 | async-start | bytes 31850496 | tf_op jit(solution)/shard_map/all_gather | solution.py:47
  8.4 7.5 %copy-start.1 = (f32[3072]{0:T(1024)S(1)}, f32[3072]{0:T(1024)}, u32[]{:S(2)}) copy-start(f32[3072]{0:T(1024)} %param.5) | copy-start | bytes 36868
  28.4 11.3 %copy-start.2 = (s32[12]{0:T(128)S(1)}, s32[12]{0:T(128)}, u32[]{:S(2)}) copy-start(s32[12]{0:T(128)} %param.7) | copy-start | bytes 148
  28.4 83.2 %all-to-all-start = ((bf16[2,256,3072]{2,0,1:T(2,128)(2,1)}), bf16[2,256,3072]{2,0,1:T(2,128)(2,1)S(1)}, u32[]{:S(2)}, u32[]{:S(2)}) async-start(bf16[2,256,3072]{2,0,1:T(2,128)(2,1)} %fusion.6), calls=%async_computation | async-start | bytes 6291456 | tf_op jit(solution)/shard_map/all_to_all | solution.py:45
Sparse Core Ops, SparseCore 0:
  10.0 333.4 all-gather.1
where the time goes:
time: 425 us
  waiting for transfers between devices  303 us (71%)
  blocking collectives  47.8 us (11%)
  matrix products  22.2 us (5%)
  other arithmetic  21.3 us (5%)
  between operations  13.5 us (3%)
  starting transfers between devices  11.3 us (3%)
  local copies, waits for them, and re-layouts  5.3 us (1%)
    all_gather x1, waiting for transfers between devices, per_device(): piece = lax.all_gather(w_qkv, 'narrow', axis=1, tiled=True)  231 us
    all_to_all x1, waiting for transfers between devices, per_device(): lax.all_to_all(normed, 'wide', split_axis=1, concat_axis=0, tiled=True)  71.7 us
    all_to_all x1, blocking collectives, per_device(): lax.all_to_all(result, 'wide', split_axis=0, concat_axis=1, tiled=True)  47.8 us
    dot_general x1, matrix products, per_device(): jnp.dot(moved.reshape(-1, width), piece, preferred_element_type=jnp.float32)  18.9 us
    convert_element_type x1, other arithmetic, normalize(): return (centered * lax.rsqrt(spread + EPS) * gain).astype(jnp.bfloat16)  12.4 us
    all_to_all x1, starting transfers between devices, per_device(): lax.all_to_all(normed, 'wide', split_axis=1, concat_axis=0, tiled=True)  11.3 us
  transfers between devices with their start and end apart: 2, of which 2 were waited for; matrix products, arithmetic and copies ran while one was open for 5% of the time, Pallas kernels for 0%

commit v1 on v0

v1 whole, which is shorter than its diff:
```python
import math

import jax
import jax.numpy as jnp
from jax import lax
from jax.experimental import pallas as pl
from jax.experimental.pallas import tpu as pltpu
from jax.sharding import Mesh, PartitionSpec as P

HD = 128
INNER = 1536
WIDTH = 3072
HALF = 1536
EPS = 1e-06
SIZES = (8, 2, 2, 2, 4)
NAMES = ("z", "yl", "c", "yh", "x")
WIDE = ("z", "yl", "c")
GROUPS = ((0,), (1, 7), (2, 6), (3, 5), (4,))


def normalize(tokens, gain):
    values = tokens.astype(jnp.float32)
    centered = values - jnp.mean(values, axis=-1, keepdims=True)
    spread = jnp.mean(centered * centered, axis=-1, keepdims=True)
    return (centered * lax.rsqrt(spread + EPS) * gain).astype(jnp.bfloat16)


def send(value, move):
    pairs = []
    for i in range(256):
        z, yl, c, yh, x = i // 32, i // 16 % 2, i // 8 % 2, i // 4 % 2, i % 4
        z, yl, c, yh, x = move(z, yl, c, yh, x)
        pairs.append((i, (((z * 2 + yl) * 2 + c) * 2 + yh) * 4 + x))
    return lax.ppermute(value, NAMES, pairs)


def right(v):
    return send(v, lambda z, yl, c, yh, x: (z, yl, c, yh, (x + 1) % 4))


def left(v):
    return send(v, lambda z, yl, c, yh, x: (z, yl, c, yh, (x + 3) % 4))


def outer(v):
    return send(v, lambda z, yl, c, yh, x: (z, 1 - yl, c, 1 - yh, x))


def inner(v):
    return send(v, lambda z, yl, c, yh, x: (z, 1 - yl, c, yh, x))


def other_core(v):
    return send(v, lambda z, yl, c, yh, x: (z, yl, 1 - c, yh, x))


def shifted(v, k):
    return send(v, lambda z, yl, c, yh, x: ((z + k) % 8, yl, c, yh, x))


def after(value, *done):
    return lax.optimization_barrier((value,) + done)[0]


def weights(w, yl, c, yh, x):
    n = yh * 4 + x
    kind = yl ^ yh
    wt = w.T

    def unit(group):
        place = n + (n >= 1 + 2 * group).astype(jnp.int32)
        row = 64 * (2 * (4 * place + group) - 9 * n)
        return lax.dynamic_slice(wt, (row, c * HALF), (128, HALF))

    second = unit(kind + 2)
    extra = lax.dynamic_slice(wt, (512 * (1 - n % 2), c * HALF), (64, HALF))
    own = jnp.concatenate([unit(kind), extra], axis=0)
    members = [
        [(((p ^ b) * 2 + k) * 2 + b) * 4 + a for b in range(2) for a in range(4)] for p in range(2) for k in range(2)
    ]
    whole = lax.all_gather(own, ("yl", "c", "yh", "x"), axis_index_groups=members, axis=0)
    far = outer(second)
    lx, rx = right(second), left(second)
    o0, o1 = right(lx[:64]), left(rx[64:])
    ready = after(far, o0, o1)
    fl, fr = right(ready), left(ready)
    f0, f1 = right(fl[:64]), left(fr[64:])
    near, away = yh * 4, (1 - yh) * 4
    l, r, o = (x + 3) % 4, (x + 1) % 4, (x + 2) % 4
    two = jnp.zeros((8, 128, HALF), jnp.bfloat16)
    for v, at, row in (
        (second, near + x, 0),
        (lx, near + l, 0),
        (rx, near + r, 0),
        (o0, near + o, 0),
        (o1, near + o, 64),
        (far, away + x, 0),
        (fl, away + l, 0),
        (fr, away + r, 0),
        (f0, away + o, 0),
        (f1, away + o, 64),
    ):
        two = lax.dynamic_update_slice(two, v[None], (at, row, 0))

    def pick(core):
        main = jnp.where(core == 0, whole[:, :128], two)
        rest = lax.dynamic_slice(whole, (2 * (kind + 2 * core), 128, 0), (2, 64, HALF)).reshape(1, 128, HALF)
        spot = 1 + 2 * (kind + 2 * core)
        j = jnp.arange(9, dtype=jnp.int32)[:, None, None]
        early = jnp.concatenate([main, rest], axis=0)
        late = jnp.concatenate([rest, main], axis=0)
        return jnp.where(j < spot, early, jnp.where(j == spot, rest, late))

    got = other_core(pick(1 - c)).reshape(1152, HALF)
    mine = pick(c).reshape(1152, HALF)
    return jnp.concatenate([jnp.where(c == 0, mine, got), jnp.where(c == 0, got, mine)], axis=1), far


def attend(qkv, band, frame):
    q, k, v = (qkv[:, 384 * i : 384 * i + 384].reshape(64, 32, 3, HD) for i in range(3))
    scores = jnp.einsum("tbhe,ubhe->bhtu", q, k, preferred_element_type=jnp.float32) * (1.0 / math.sqrt(HD))
    distance = jnp.abs(frame[:, None] - frame[None, :])
    allowed = distance[None, None, :, :] <= band[None, :, None, None]
    scores = jnp.where(allowed, scores, -jnp.inf)
    highest = jnp.max(scores, axis=-1, keepdims=True)
    e = jnp.exp(scores - highest)
    total = jnp.sum(e, axis=-1, keepdims=True)
    probs = (e / total).astype(jnp.bfloat16)
    result = jnp.einsum("bhtu,ubhe->tbhe", probs, v, preferred_element_type=jnp.float32)
    return result.astype(jnp.bfloat16).reshape(32, 64, 384)


def reorder(blocks, order):
    def kernel(order_ref, in_ref, out_ref):
        def body(i, carry):
            out_ref[i] = in_ref[order_ref[i]]
            return carry

        lax.fori_loop(0, 32, body, 0)

    return pl.pallas_call(
        kernel,
        out_shape=jax.ShapeDtypeStruct((32, 64, 384), jnp.bfloat16),
        in_specs=[pl.BlockSpec(memory_space=pltpu.SMEM), pl.BlockSpec(memory_space=pltpu.VMEM)],
        out_specs=pl.BlockSpec(memory_space=pltpu.VMEM),
        compiler_params=pltpu.CompilerParams(vmem_limit_bytes=16 * 2**20),
        name="reorder",
    )(order, blocks)


def spread(blocks, source):
    def kernel(source_ref, in_ref, out_ref):
        def body(z, carry):
            rows = pl.ds(pl.multiple_of(z * 32, 32), 32)
            for g in range(4):
                w = z * 4 + source_ref[g]
                for f in range(2):
                    for i in range(3):
                        column = (4 * i + g) * HD
                        out_ref[f, rows, column : column + HD] = in_ref[w, f * 32 : f * 32 + 32, i * HD : i * HD + HD]
            return carry

        lax.fori_loop(0, 8, body, 0)

    return pl.pallas_call(
        kernel,
        out_shape=jax.ShapeDtypeStruct((2, 256, INNER), jnp.bfloat16),
        in_specs=[pl.BlockSpec(memory_space=pltpu.SMEM), pl.BlockSpec(memory_space=pltpu.VMEM)],
        out_specs=pl.BlockSpec(memory_space=pltpu.VMEM),
        compiler_params=pltpu.CompilerParams(vmem_limit_bytes=16 * 2**20),
        name="spread",
    )(source, blocks)


def per_device(tokens, gain, w_qkv, band):
    z, yl, c, yh, x = (lax.axis_index(n) for n in NAMES)
    w, first = weights(w_qkv, yl, c, yh, x)
    normed = normalize(tokens, gain).reshape(2, 8, 32, WIDTH)

    def block(k):
        to = (z + k) % 8
        return lax.dynamic_slice(normed, (0, to, 0, 0), (2, 1, 32, WIDTH)).reshape(64, WIDTH)

    outs, frames, owners = [], [], []
    came = ()
    for group in GROUPS:
        if group[0] == 0:
            here = after(block(0), first)
        else:
            came = tuple(shifted(after(block(k), *came), k) for k in group)
            here = jnp.concatenate(came, axis=0)
        pair = jnp.concatenate([here, inner(here)], axis=0)
        four = jnp.concatenate([pair, other_core(pair)], axis=0)
        y = lax.dot_general(four, w, (((1,), (1,)), ((), ())), preferred_element_type=jnp.float32)
        outs.append(y.astype(jnp.bfloat16))
        for b in range(2):
            for a in range(2):
                for k in group:
                    owner = ((z - k) % 8) * 4 + (yl ^ a) * 2 + (c ^ b)
                    owners.append(owner)
                    frames += [owner * 2, owner * 2 + 1]
    kind = yl ^ yh
    mine = lax.dynamic_slice(band.reshape(3, 4), (0, kind + 2 * c), (3, 1)).reshape(3)
    result = attend(jnp.concatenate(outs, axis=0), mine, jnp.stack(frames))
    w = jnp.arange(32, dtype=jnp.int32)
    order = jnp.sum(jnp.where(jnp.stack(owners)[None, :] == w[:, None], w[None, :], 0), axis=1)
    back = lax.all_to_all(reorder(result, order), WIDE, 0, 0, tiled=True)
    g = jnp.arange(4, dtype=jnp.int32)
    return spread(back, ((g % 2) ^ yh) * 2 + g // 2)


def solution(mesh):
    own = Mesh(mesh.devices.reshape(SIZES), NAMES)
    tok = P(WIDE, ("yh", "x"), None)
    placed = (tok, P(), P(None, ("yh", "x")), P())
    return jax.shard_map(per_device, mesh=own, in_specs=placed, out_specs=tok, check_vma=False)
```

time: 425 us -> 307 us (0.72); the launches traced: 425 us -> 302 us
  waiting for transfers between devices: 303 us -> 134 us
  starting transfers between devices: 11.3 us -> 62.3 us
  blocking collectives: 47.8 us -> 0 us
  local copies, waits for them, and re-layouts: 5.3 us -> 37.9 us
  matrix products: 22.2 us -> 28.6 us
    all_gather x1, waiting for transfers between devices: 231 us -> 17.2 us  [weights(): lax.all_gather(own, ('yl', 'c', 'yh', 'x'), axis_index_groups=members, ax...]
    ppermute x0 -> x27, waiting for transfers between devices: none -> 77.4 us  [send(): return lax.ppermute(value, NAMES, pairs)]
    ppermute x0 -> x27, starting transfers between devices: none -> 54.1 us  [send(): return lax.ppermute(value, NAMES, pairs)]
    all_to_all x1 -> x0, blocking collectives: 47.8 us -> none  [per_device(): lax.all_to_all(result, 'wide', split_axis=0, concat_axis=1, tiled=True)]
    all_to_all x1, waiting for transfers between devices: 71.7 us -> 39.2 us  [per_device(): back = lax.all_to_all(reorder(result, order), WIDE, 0, 0, tiled=True)]
    reshape x1 -> x5, local copies, waits for them, and re-layouts: 0.81 us -> 18.4 us  [the longest x3 14.4 us: attend(): qkv[:, 384 * i:384 * i + 384].reshape(64, 32, 3, HD)]
    convert_element_type x1, other arithmetic: 12.4 us -> 1.61 us  [normalize(): return (centered * lax.rsqrt(spread + EPS) * gain).astype(jnp.bfloat16)]
    concatenate x0 -> x10, other arithmetic: none -> 8.49 us  [the longest x5 4.55 us: per_device(): pair = jnp.concatenate([here, inner(here)], axis=0)]
  transfers between devices with their start and end apart: 2 -> 29, of which waited for: 2 -> 12; matrix products, arithmetic and copies ran while one was open for 5% -> 17% of each run, Pallas kernels for 0% -> 0%
where the time goes in v1:
time: 307 us; the launch traced here: 302 us
  waiting for transfers between devices  134 us (44%)
  starting transfers between devices  62.3 us (20%)
  local copies, waits for them, and re-layouts  37.9 us (12%)
  matrix products  28.6 us (9%)
  other arithmetic  21.4 us (7%)
  between operations  14.2 us (5%)
  Pallas kernels  4.09 us (1%)
    ppermute x27, waiting for transfers between devices, send(): return lax.ppermute(value, NAMES, pairs)  77.4 us
    ppermute x27, starting transfers between devices, send(): return lax.ppermute(value, NAMES, pairs)  54.1 us
    all_to_all x1, waiting for transfers between devices, per_device(): back = lax.all_to_all(reorder(result, order), WIDE, 0, 0, tiled=True)  39.2 us
    dot_general x5, matrix products, per_device(): lax.dot_general(four, w, (((1,), (1,)), ((), ())), preferred_element_type...  22.1 us
    all_gather x1, waiting for transfers between devices, weights(): lax.all_gather(own, ('yl', 'c', 'yh', 'x'), axis_index_groups=members, ax...  17.2 us
    reshape x3, local copies, waits for them, and re-layouts, attend(): qkv[:, 384 * i:384 * i + 384].reshape(64, 32, 3, HD)  14.4 us
    all_to_all x1, starting transfers between devices, per_device(): back = lax.all_to_all(reorder(result, order), WIDE, 0, 0, tiled=True)  8.2 us
  transfers between devices with their start and end apart: 29, of which 12 were waited for; matrix products, arithmetic and copies ran while one was open for 17% of the time, Pallas kernels for 0%

profile of v1, /device:TPU:1, one launch (start us, length us, event | category | flops | bytes accessed | tf_op | source)
XLA Modules:
  0.0 302.3 jit_solution(2210402943032235574)
XLA Ops:
  10.5 3.7 %collective-permute-start = (bf16[128,1536]{1,0:T(8,128)(2,1)}, bf16[128,1536]{1,0:T(8,128)(2,1)}, u32[]{:S(2)}, u32[]{:S(2)}) collective-permute-start(bf16[128,1536]{1,0:T(8,128)(2,1)} %get-tuple-element.31), channel_id=1, source_target_pairs={{0,20},{1,21},{2,22},{3,23},{4,16},{5,17},{6,18},{7,19},{8,28},{9,... | collective-permute-start | bytes 1179656 | tf_op jit(solution)/shard_map/ppermute | solution.py:34
  21.7 5.6 %collective-permute-start.13 = (bf16[64,3072]{1,0:T(8,128)(2,1)}, bf16[64,3072]{1,0:T(8,128)(2,1)S(1)}, u32[]{:S(2)}, u32[]{:S(2)}) collective-permute-start(bf16[64,3072]{1,0:T(8,128)(2,1)} %bitcast.59), channel_id=1, source_target_pairs={{0,224},{1,225},{2,226},{3,227},{4,228},{5,229},{6,230},{7,231},{8... | collective-permute-start | bytes 1179656 | tf_op jit(solution)/shard_map/ppermute | solution.py:34
  47.8 16.2 %collective-permute-done.7 = bf16[128,1536]{1,0:T(8,128)(2,1)S(1)} collective-permute-done((bf16[128,1536]{1,0:T(8,128)(2,1)}, bf16[128,1536]{1,0:T(8,128)(2,1)S(1)}, u32[]{:S(2)}, u32[]{:S(2)}) %collective-permute-start.7) | collective-permute-done | bytes 393248 | tf_op jit(solution)/shard_map/ppermute | solution.py:34
  66.9 8.3 %collective-permute-done.9 = bf16[64,1536]{1,0:T(8,128)(2,1)S(1)} collective-permute-done((bf16[64,1536]{1,0:T(8,128)(2,1)S(1)}, bf16[64,1536]{1,0:T(8,128)(2,1)S(1)}, u32[]{:S(2)}, u32[]{:S(2)}) %collective-permute-start.9) | collective-permute-done | bytes 196640 | tf_op jit(solution)/shard_map/ppermute | solution.py:34
  75.3 17.2 %all-gather.3.cloned.1.call-done = bf16[1536,1536]{1,0:T(8,128)(2,1)} async-done(((bf16[192,1536]{1,0:T(8,128)(2,1)}), bf16[1536,1536]{1,0:T(8,128)(2,1)}) %all-gather.3.cloned.1.call-update) | async-done | bytes 4718608 | tf_op jit(solution)/shard_map/all_gather | solution.py:81
  94.5 4.0 %broadcast_select_fusion.1 = (bf16[8,128,1536]{2,1,0:T(8,128)(2,1)}, bf16[8,128,1536]{2,1,0:T(8,128)(2,1)S(1)}) fusion(bf16[8,128,1536]{2,1,0:T(8,128)(2,1)S(1)} %bitcast_dynamic-update-slice_fusion.6, pred[]{:T(512)S(6)} %eq.89, bf16[8,192,1536]{2,1,0:T(8,128)(2,1)} %bitcast.172, pred[]{:T(512)S(6)} %eq.91), kind=kLoop, calls=%fused_computation.45 | loop fusion | flops 3145728 | bytes 12582914 | tf_op jit(solution)/shard_map/jit(_where)/select_n | solution.py:106
  100.5 4.7 %collective-permute-start.21 = (bf16[64,3072]{1,0:T(8,128)(2,1)}, bf16[64,3072]{1,0:T(8,128)(2,1)S(1)}, u32[]{:S(2)}, u32[]{:S(2)}) collective-permute-start(bf16[64,3072]{1,0:T(8,128)(2,1)} %bitcast.178), channel_id=1, source_target_pairs={{0,160},{1,161},{2,162},{3,163},{4,164},{5,165},{6,166},{7,167},{8... | collective-permute-start | bytes 1179656 | tf_op jit(solution)/shard_map/ppermute | solution.py:34
  109.0 21.8 %collective-permute-done.21 = bf16[64,3072]{1,0:T(8,128)(2,1)S(1)} collective-permute-done((bf16[64,3072]{1,0:T(8,128)(2,1)}, bf16[64,3072]{1,0:T(8,128)(2,1)S(1)}, u32[]{:S(2)}, u32[]{:S(2)}) %collective-permute-start.21) | collective-permute-done | bytes 393248 | tf_op jit(solution)/shard_map/ppermute | solution.py:34
  132.0 3.7 %collective-permute-done.20 = bf16[64,3072]{1,0:T(8,128)(2,1)S(1)} collective-permute-done((bf16[64,3072]{1,0:T(8,128)(2,1)}, bf16[64,3072]{1,0:T(8,128)(2,1)S(1)}, u32[]{:S(2)}, u32[]{:S(2)}) %collective-permute-start.20) | collective-permute-done | bytes 393248 | tf_op jit(solution)/shard_map/ppermute | solution.py:34
  139.5 9.3 %collective-permute-done.18 = bf16[128,3072]{1,0:T(8,128)(2,1)S(1)} collective-permute-done((bf16[128,3072]{1,0:T(8,128)(2,1)S(1)}, bf16[128,3072]{1,0:T(8,128)(2,1)S(1)}, u32[]{:S(2)}, u32[]{:S(2)}) %collective-permute-start.18) | collective-permute-done | bytes 786464 | tf_op jit(solution)/shard_map/ppermute | solution.py:34
  152.3 5.3 %collective-permute-done.24 = bf16[64,3072]{1,0:T(8,128)(2,1)S(1)} collective-permute-done((bf16[64,3072]{1,0:T(8,128)(2,1)S(1)}, bf16[64,3072]{1,0:T(8,128)(2,1)S(1)}, u32[]{:S(2)}, u32[]{:S(2)}) %collective-permute-start.24) | collective-permute-done | bytes 393248 | tf_op jit(solution)/shard_map/ppermute | solution.py:34
  161.4 4.3 %collective-permute-done.22 = bf16[128,3072]{1,0:T(8,128)(2,1)S(1)} collective-permute-done((bf16[128,3072]{1,0:T(8,128)(2,1)S(1)}, bf16[128,3072]{1,0:T(8,128)(2,1)S(1)}, u32[]{:S(2)}, u32[]{:S(2)}) %collective-permute-start.22) | collective-permute-done | bytes 786464 | tf_op jit(solution)/shard_map/ppermute | solution.py:34
  169.3 4.8 %collective-permute-done.25 = bf16[64,3072]{1,0:T(8,128)(2,1)S(1)} collective-permute-done((bf16[64,3072]{1,0:T(8,128)(2,1)S(1)}, bf16[64,3072]{1,0:T(8,128)(2,1)S(1)}, u32[]{:S(2)}, u32[]{:S(2)}) %collective-permute-start.25) | collective-permute-done | bytes 393248 | tf_op jit(solution)/shard_map/ppermute | solution.py:34
  177.7 9.5 %collective-permute-start.26 = (bf16[128,3072]{1,0:T(8,128)(2,1)}, bf16[128,3072]{1,0:T(8,128)(2,1)S(1)}, u32[]{:S(2)}, u32[]{:S(2)}) collective-permute-start(bf16[128,3072]{1,0:T(8,128)(2,1)} %pad_maximum_fusion.10), channel_id=1, source_target_pairs={{0,8},{1,9},{2,10},{3,11},{4,12},{5,13},{6,14},{7,15},{8,0},{9,1},... | collective-permute-start | bytes 2359304 | tf_op jit(solution)/shard_map/ppermute | solution.py:34
  192.1 5.9 %fusion.46 = bf16[2048,1152]{1,0:T(8,128)(2,1)S(1)} fusion(bf16[2048,1152]{1,0:T(8,128)(2,1)S(1)} %fusion.50, bf16[256,3072]{1,0:T(8,128)(2,1)} %collective-permute-done.15, bf16[128,3072]{1,0:T(8,128)(2,1)S(1)} %copy-done.16, bf16[64,3072]{1,0:T(8,128)(2,1)S(1)} %copy-done.5, bf16[64,3072]{1,0:T(8,128)(2,1)} %collective-permute-done.12, ...), kind=kOutput, calls=%fused_computation.51 | convolution fusion | flops 3651207168 | bytes 11403264 | tf_op jit(solution)/shard_map/dot_general | solution.py:194
  198.1 6.0 %fusion.40 = bf16[2048,1152]{1,0:T(8,128)(2,1)S(1)} fusion(bf16[2048,1152]{1,0:T(8,128)(2,1)S(1)} %fusion.46, bf16[256,3072]{1,0:T(8,128)(2,1)} %collective-permute-done.19, bf16[128,3072]{1,0:T(8,128)(2,1)S(1)} %copy-done.14, bf16[64,3072]{1,0:T(8,128)(2,1)} %collective-permute-done.17, bf16[64,3072]{1,0:T(8,128)(2,1)} %collective-permute-done.16, ...), kind=kOutput, calls=%fused_computation.49 | convolution fusion | flops 3651207168 | bytes 11403264 | tf_op jit(solution)/shard_map/dot_general | solution.py:194
  204.1 5.8 %fusion.34 = bf16[2048,1152]{1,0:T(8,128)(2,1)S(1)} fusion(bf16[2048,1152]{1,0:T(8,128)(2,1)S(1)} %fusion.40, bf16[256,3072]{1,0:T(8,128)(2,1)} %collective-permute-done.23, bf16[128,3072]{1,0:T(8,128)(2,1)S(1)} %copy-done.12, bf16[64,3072]{1,0:T(8,128)(2,1)S(1)} %copy-done.7, bf16[64,3072]{1,0:T(8,128)(2,1)S(1)} %copy-done.9, ...), kind=kOutput, calls=%fused_computation.47 | convolution fusion | flops 3651207168 | bytes 11403264 | tf_op jit(solution)/shard_map/dot_general | solution.py:194
  214.6 4.1 %reshape.145 = bf16[64,32,3,128]{3,2,1,0:T(4,128)(2,1)S(1)} reshape(bf16[2048,384]{1,0:T(8,128)(2,1)} %get-tuple-element.24) | data formatting | bytes 3145728 | tf_op jit(solution)/shard_map/reshape | solution.py:120
  218.7 5.1 %reshape.144 = bf16[64,32,3,128]{3,2,1,0:T(4,128)(2,1)} reshape(bf16[2048,384]{1,0:T(8,128)(2,1)} %get-tuple-element.25) | data formatting | bytes 3145728 | tf_op jit(solution)/shard_map/reshape | solution.py:120
  223.8 5.1 %reshape.142 = bf16[64,32,3,128]{3,2,1,0:T(4,128)(2,1)} reshape(bf16[2048,384]{1,0:T(8,128)(2,1)} %get-tuple-element.23) | data formatting | bytes 3145728 | tf_op jit(solution)/shard_map/reshape | solution.py:120
  229.0 4.6 %fusion.63 = f32[32,3,64,64]{2,3,1,0:T(8,128)S(1)} fusion(bf16[64,32,3,128]{3,2,1,0:T(4,128)(2,1)S(1)} %reshape.145, bf16[64,32,3,128]{3,2,1,0:T(4,128)(2,1)} %reshape.144), kind=kOutput, calls=%fused_computation.72 | convolution fusion | flops 100663296 | bytes 4718592 | tf_op jit(solution)/shard_map/tbhe,ubhe->bhtu/dot_general | solution.py:121
  239.8 4.0 %reshape.146.in_ref = bf16[32,64,384]{2,1,0:T(8,128)(2,1)S(1)} reshape(bf16[64,32,3,128]{3,2,1,0:T(4,128)(2,1)} %copy.19) | data formatting | bytes 3145728 | tf_op jit(solution)/shard_map/reshape | solution.py:130
  245.8 8.2 %all-to-all-start = ((bf16[32,64,384]{2,1,0:T(8,128)(2,1)}), bf16[32,64,384]{2,1,0:T(8,128)(2,1)S(1)}, u32[]{:S(2)}, u32[]{:S(2)}) async-start(bf16[32,64,384]{2,1,0:T(8,128)(2,1)} %reorder.1), calls=%async_computation | async-start | bytes 3145728 | tf_op jit(solution)/shard_map/all_to_all | solution.py:207
  254.0 39.2 %all-to-all-done.in_ref = bf16[32,64,384]{2,1,0:T(8,128)(2,1)S(1)} async-done(((bf16[32,64,384]{2,1,0:T(8,128)(2,1)}), bf16[32,64,384]{2,1,0:T(8,128)(2,1)S(1)}, u32[]{:S(2)}, u32[]{:S(2)}) %all-to-all-start) | async-done | bytes 1572896 | tf_op jit(solution)/shard_map/all_to_all | solution.py:207
  (152 shorter events, 81.6 us)
Async XLA Ops:
  6.5 86.0 %all-gather.3.cloned.1.call-start = ((), (), s32[]{:S(2)}) async-start(), calls=%async_computation.1 | async-start | bytes 5308416 | tf_op jit(solution)/shard_map/all_gather | solution.py:81
  10.5 31.5 %collective-permute-start = (bf16[128,1536]{1,0:T(8,128)(2,1)}, bf16[128,1536]{1,0:T(8,128)(2,1)}, u32[]{:S(2)}, u32[]{:S(2)}) collective-permute-start(bf16[128,1536]{1,0:T(8,128)(2,1)} %get-tuple-element.31), channel_id=1, source_target_pairs={{0,20},{1,21},{2,22},{3,23},{4,16},{5,17},{6,18},{7,19},{8,28},{9,... | collective-permute-start | bytes 1179656 | tf_op jit(solution)/shard_map/ppermute | solution.py:34
  14.1 16.2 %collective-permute-start.3 = (bf16[128,1536]{1,0:T(8,128)(2,1)}, bf16[128,1536]{1,0:T(8,128)(2,1)}, u32[]{:S(2)}, u32[]{:S(2)}) collective-permute-start(bf16[128,1536]{1,0:T(8,128)(2,1)} %get-tuple-element.31), channel_id=1, source_target_pairs={{0,1},{1,2},{2,3},{3,0},{4,5},{5,6},{6,7},{7,4},{8,9},{9,10},{10,1... | collective-permute-start | bytes 1179656 | tf_op jit(solution)/shard_map/ppermute | solution.py:34
  15.3 16.1 %collective-permute-start.4 = (bf16[128,1536]{1,0:T(8,128)(2,1)}, bf16[128,1536]{1,0:T(8,128)(2,1)}, u32[]{:S(2)}, u32[]{:S(2)}) collective-permute-start(bf16[128,1536]{1,0:T(8,128)(2,1)} %get-tuple-element.31), channel_id=1, source_target_pairs={{0,3},{1,0},{2,1},{3,2},{4,7},{5,4},{6,5},{7,6},{8,11},{9,8},{10,9... | collective-permute-start | bytes 1179656 | tf_op jit(solution)/shard_map/ppermute | solution.py:34
  21.7 13.4 %collective-permute-start.13 = (bf16[64,3072]{1,0:T(8,128)(2,1)}, bf16[64,3072]{1,0:T(8,128)(2,1)S(1)}, u32[]{:S(2)}, u32[]{:S(2)}) collective-permute-start(bf16[64,3072]{1,0:T(8,128)(2,1)} %bitcast.59), channel_id=1, source_target_pairs={{0,224},{1,225},{2,226},{3,227},{4,228},{5,229},{6,230},{7,231},{8... | collective-permute-start | bytes 1179656 | tf_op jit(solution)/shard_map/ppermute | solution.py:34
  37.6 62.9 %collective-permute-start.17 = (bf16[64,3072]{1,0:T(8,128)(2,1)}, bf16[64,3072]{1,0:T(8,128)(2,1)}, u32[]{:S(2)}, u32[]{:S(2)}) collective-permute-start(bf16[64,3072]{1,0:T(8,128)(2,1)} %bitcast.61), channel_id=1, source_target_pairs={{0,192},{1,193},{2,194},{3,195},{4,196},{5,197},{6,198},{7,199},{8... | collective-permute-start | bytes 1179656 | tf_op jit(solution)/shard_map/ppermute | solution.py:34
  37.6 62.9 %collective-permute-start.16 = (bf16[64,3072]{1,0:T(8,128)(2,1)}, bf16[64,3072]{1,0:T(8,128)(2,1)}, u32[]{:S(2)}, u32[]{:S(2)}) collective-permute-start(bf16[64,3072]{1,0:T(8,128)(2,1)} %bitcast.60), channel_id=1, source_target_pairs={{0,64},{1,65},{2,66},{3,67},{4,68},{5,69},{6,70},{7,71},{8,72},{9,... | collective-permute-start | bytes 1179656 | tf_op jit(solution)/shard_map/ppermute | solution.py:34
  43.1 20.9 %collective-permute-start.7 = (bf16[128,1536]{1,0:T(8,128)(2,1)}, bf16[128,1536]{1,0:T(8,128)(2,1)S(1)}, u32[]{:S(2)}, u32[]{:S(2)}) collective-permute-start(bf16[128,1536]{1,0:T(8,128)(2,1)} %collective-permute-done), channel_id=1, source_target_pairs={{0,1},{1,2},{2,3},{3,0},{4,5},{5,6},{6,7},{7,4},{8,9},{9,10},{10,1... | collective-permute-start | bytes 1179656 | tf_op jit(solution)/shard_map/ppermute | solution.py:34
  44.2 19.9 %collective-permute-start.8 = (bf16[128,1536]{1,0:T(8,128)(2,1)}, bf16[128,1536]{1,0:T(8,128)(2,1)S(1)}, u32[]{:S(2)}, u32[]{:S(2)}) collective-permute-start(bf16[128,1536]{1,0:T(8,128)(2,1)} %collective-permute-done), channel_id=1, source_target_pairs={{0,3},{1,0},{2,1},{3,2},{4,7},{5,4},{6,5},{7,6},{8,11},{9,8},{10,9... | collective-permute-start | bytes 1179656 | tf_op jit(solution)/shard_map/ppermute | solution.py:34
  99.3 78.4 %collective-permute-start.11 = (bf16[9,128,1536]{2,1,0:T(8,128)(2,1)S(1)}, bf16[9,128,1536]{2,1,0:T(8,128)(2,1)}, u32[]{:S(2)}, u32[]{:S(2)}) collective-permute-start(bf16[9,128,1536]{2,1,0:T(8,128)(2,1)S(1)} %maximum_select_fusion), channel_id=1, source_target_pairs={{0,8},{1,9},{2,10},{3,11},{4,12},{5,13},{6,14},{7,15},{8,0},{9,1},... | collective-permute-start | bytes 10616840 | tf_op jit(solution)/shard_map/ppermute | solution.py:34
  100.3 36.9 %collective-permute-start.1 = (bf16[64,3072]{1,0:T(8,128)(2,1)}, bf16[64,3072]{1,0:T(8,128)(2,1)S(1)}, u32[]{:S(2)}, u32[]{:S(2)}) collective-permute-start(bf16[64,3072]{1,0:T(8,128)(2,1)} %bitcast.173), channel_id=1, source_target_pairs={{0,16},{1,17},{2,18},{3,19},{4,20},{5,21},{6,22},{7,23},{8,24},{9,... | collective-permute-start | bytes 1179656 | tf_op jit(solution)/shard_map/ppermute | solution.py:34
  100.5 30.4 %collective-permute-start.21 = (bf16[64,3072]{1,0:T(8,128)(2,1)}, bf16[64,3072]{1,0:T(8,128)(2,1)S(1)}, u32[]{:S(2)}, u32[]{:S(2)}) collective-permute-start(bf16[64,3072]{1,0:T(8,128)(2,1)} %bitcast.178), channel_id=1, source_target_pairs={{0,160},{1,161},{2,162},{3,163},{4,164},{5,165},{6,166},{7,167},{8... | collective-permute-start | bytes 1179656 | tf_op jit(solution)/shard_map/ppermute | solution.py:34
  105.2 30.5 %collective-permute-start.20 = (bf16[64,3072]{1,0:T(8,128)(2,1)}, bf16[64,3072]{1,0:T(8,128)(2,1)S(1)}, u32[]{:S(2)}, u32[]{:S(2)}) collective-permute-start(bf16[64,3072]{1,0:T(8,128)(2,1)} %bitcast.177), channel_id=1, source_target_pairs={{0,96},{1,97},{2,98},{3,99},{4,100},{5,101},{6,102},{7,103},{8,104... | collective-permute-start | bytes 1179656 | tf_op jit(solution)/shard_map/ppermute | solution.py:34
  106.4 30.9 %collective-permute-start.14 = (bf16[128,3072]{1,0:T(8,128)(2,1)S(1)}, bf16[128,3072]{1,0:T(8,128)(2,1)S(1)}, u32[]{:S(2)}, u32[]{:S(2)}) collective-permute-start(bf16[128,3072]{1,0:T(8,128)(2,1)S(1)} %pad_maximum_fusion.7), channel_id=1, source_target_pairs={{0,16},{1,17},{2,18},{3,19},{4,20},{5,21},{6,22},{7,23},{8,24},{9,... | collective-permute-start | bytes 2359304 | tf_op jit(solution)/shard_map/ppermute | solution.py:34
  130.8 18.0 %collective-permute-start.18 = (bf16[128,3072]{1,0:T(8,128)(2,1)S(1)}, bf16[128,3072]{1,0:T(8,128)(2,1)S(1)}, u32[]{:S(2)}, u32[]{:S(2)}) collective-permute-start(bf16[128,3072]{1,0:T(8,128)(2,1)S(1)} %pad_maximum_fusion.8), channel_id=1, source_target_pairs={{0,16},{1,17},{2,18},{3,19},{4,20},{5,21},{6,22},{7,23},{8,24},{9,... | collective-permute-start | bytes 2359304 | tf_op jit(solution)/shard_map/ppermute | solution.py:34
  135.7 29.9 %collective-permute-start.22 = (bf16[128,3072]{1,0:T(8,128)(2,1)S(1)}, bf16[128,3072]{1,0:T(8,128)(2,1)S(1)}, u32[]{:S(2)}, u32[]{:S(2)}) collective-permute-start(bf16[128,3072]{1,0:T(8,128)(2,1)S(1)} %pad_maximum_fusion.9), channel_id=1, source_target_pairs={{0,16},{1,17},{2,18},{3,19},{4,20},{5,21},{6,22},{7,23},{8,24},{9,... | collective-permute-start | bytes 2359304 | tf_op jit(solution)/shard_map/ppermute | solution.py:34
  137.3 20.4 %collective-permute-start.24 = (bf16[64,3072]{1,0:T(8,128)(2,1)S(1)}, bf16[64,3072]{1,0:T(8,128)(2,1)S(1)}, u32[]{:S(2)}, u32[]{:S(2)}) collective-permute-start(bf16[64,3072]{1,0:T(8,128)(2,1)S(1)} %bitcast.176), channel_id=1, source_target_pairs={{0,128},{1,129},{2,130},{3,131},{4,132},{5,133},{6,134},{7,135},{8... | collective-permute-start | bytes 1179656 | tf_op jit(solution)/shard_map/ppermute | solution.py:34
  137.3 52.5 %collective-permute-start.2 = (bf16[128,3072]{1,0:T(8,128)(2,1)S(1)}, bf16[128,3072]{1,0:T(8,128)(2,1)S(1)}, u32[]{:S(2)}, u32[]{:S(2)}) collective-permute-start(bf16[128,3072]{1,0:T(8,128)(2,1)S(1)} %pad_maximum_fusion.6), channel_id=1, source_target_pairs={{0,8},{1,9},{2,10},{3,11},{4,12},{5,13},{6,14},{7,15},{8,0},{9,1},... | collective-permute-start | bytes 2359304 | tf_op jit(solution)/shard_map/ppermute | solution.py:34
  148.8 43.3 %collective-permute-start.15 = (bf16[256,3072]{1,0:T(8,128)(2,1)S(1)}, bf16[256,3072]{1,0:T(8,128)(2,1)}, u32[]{:S(2)}, u32[]{:S(2)}) collective-permute-start(bf16[256,3072]{1,0:T(8,128)(2,1)S(1)} %pad_maximum_fusion.3), channel_id=1, source_target_pairs={{0,8},{1,9},{2,10},{3,11},{4,12},{5,13},{6,14},{7,15},{8,0},{9,1},... | collective-permute-start | bytes 4718600 | tf_op jit(solution)/shard_map/ppermute | solution.py:34
  157.7 16.4 %collective-permute-start.25 = (bf16[64,3072]{1,0:T(8,128)(2,1)S(1)}, bf16[64,3072]{1,0:T(8,128)(2,1)S(1)}, u32[]{:S(2)}, u32[]{:S(2)}) collective-permute-start(bf16[64,3072]{1,0:T(8,128)(2,1)S(1)} %collective-permute-done.24), channel_id=1, source_target_pairs={{0,16},{1,17},{2,18},{3,19},{4,20},{5,21},{6,22},{7,23},{8,24},{9,... | collective-permute-start | bytes 1179656 | tf_op jit(solution)/shard_map/ppermute | solution.py:34
  165.7 32.4 %collective-permute-start.19 = (bf16[256,3072]{1,0:T(8,128)(2,1)}, bf16[256,3072]{1,0:T(8,128)(2,1)}, u32[]{:S(2)}, u32[]{:S(2)}) collective-permute-start(bf16[256,3072]{1,0:T(8,128)(2,1)} %pad_maximum_fusion.4), channel_id=1, source_target_pairs={{0,8},{1,9},{2,10},{3,11},{4,12},{5,13},{6,14},{7,15},{8,0},{9,1},... | collective-permute-start | bytes 4718600 | tf_op jit(solution)/shard_map/ppermute | solution.py:34
  174.1 30.0 %collective-permute-start.23 = (bf16[256,3072]{1,0:T(8,128)(2,1)S(1)}, bf16[256,3072]{1,0:T(8,128)(2,1)}, u32[]{:S(2)}, u32[]{:S(2)}) collective-permute-start(bf16[256,3072]{1,0:T(8,128)(2,1)S(1)} %pad_maximum_fusion.5), channel_id=1, source_target_pairs={{0,8},{1,9},{2,10},{3,11},{4,12},{5,13},{6,14},{7,15},{8,0},{9,1},... | collective-permute-start | bytes 4718600 | tf_op jit(solution)/shard_map/ppermute | solution.py:34
  177.7 32.2 %collective-permute-start.26 = (bf16[128,3072]{1,0:T(8,128)(2,1)}, bf16[128,3072]{1,0:T(8,128)(2,1)S(1)}, u32[]{:S(2)}, u32[]{:S(2)}) collective-permute-start(bf16[128,3072]{1,0:T(8,128)(2,1)} %pad_maximum_fusion.10), channel_id=1, source_target_pairs={{0,8},{1,9},{2,10},{3,11},{4,12},{5,13},{6,14},{7,15},{8,0},{9,1},... | collective-permute-start | bytes 2359304 | tf_op jit(solution)/shard_map/ppermute | solution.py:34
  245.8 47.4 %all-to-all-start = ((bf16[32,64,384]{2,1,0:T(8,128)(2,1)}), bf16[32,64,384]{2,1,0:T(8,128)(2,1)S(1)}, u32[]{:S(2)}, u32[]{:S(2)}) async-start(bf16[32,64,384]{2,1,0:T(8,128)(2,1)} %reorder.1), calls=%async_computation | async-start | bytes 3145728 | tf_op jit(solution)/shard_map/all_to_all | solution.py:207
  (31 other events, 448.1 us)
Sparse Core Ops, SparseCore 0:
  10.6 81.9 all-gather.2
